TPU v7x, 32 devices: a whole 2x2x4 slice. The times are simulated.
32 devices in a mesh: group: 2 (over y), expert: 4 (over z), tensor: 4 (over x, core).
Axes of the slice: x: 2, y: 2, z: 4, core: 2. Of those that a mesh axis runs over, the one named last changes fastest.
Arguments:
- activations: bfloat16 [1024, 7168], P(('group', 'expert'), 'tensor'), parts along dimension 0, may hold values from -6 to 6
- out_grad: bfloat16 [1024, 7168], P(('group', 'expert'), 'tensor'), parts along dimension 0, may hold values from -6 to 6
- routes: int32 [1024, 2], P(('group', 'expert')), parts along dimension 0, may hold values from 0 to 3, all different within a row; in each aligned block of 128 rows (0 to 127, 128 to 255, ...) at most 96 rows name the same one
- gates: float32 [1024, 2], P(('group', 'expert')), parts along dimension 0, may hold values from 0.1 to 1
- gate_weight: bfloat16 [4, 7168, 2048], P('expert', None, 'tensor'), may hold values from -0.0625 to 0.0625
- up_weight: bfloat16 [4, 7168, 2048], P('expert', None, 'tensor'), may hold values from -0.0625 to 0.0625
- down_weight: bfloat16 [4, 2048, 7168], P('expert', 'tensor'), may hold values from -0.125 to 0.125
Outputs:
- input_grad: bfloat16 [1024, 7168], P(('group', 'expert'), 'tensor'), parts along dimension 0
There are 2 independent parts, one for each index of `group`. A program takes and returns all parts, laid end to end along the dimension named above; an argument that names none is the same for every part. Nothing has to cross between parts.
Inputs may be any that keep to these rules, and one draw needn't show every extreme that they name: `routes`: each row names 2 different experts. Among the 128 rows of one index of expert no expert is named by more than 96 rows, a bound that some block reaches of them. Every expert is named by some row.
All inputs are finite; a program needn't handle non-finite values.
Results may differ from a plain program's by a relative error of at most 0.011.
Values may be sent and summed in bfloat16 or wider, within the bound.
A program may use at most 128 MiB of HBM per device.

v0:
```python
import jax
import jax.numpy as jnp
from jax import lax
from jax.sharding import PartitionSpec as P


def expert_grads(x_rows, d_rows, w_gate, w_up, w_down):
    pre_gate = jnp.dot(x_rows, w_gate, preferred_element_type=jnp.float32)
    pre_up = jnp.dot(x_rows, w_up, preferred_element_type=jnp.float32)
    hidden_grad = lax.dot_general(
        d_rows, w_down, (((1,), (1,)), ((), ())), preferred_element_type=jnp.float32
    )
    sigma = jax.nn.sigmoid(pre_gate)
    gate_grad = (hidden_grad * pre_up * sigma * (1.0 + pre_gate * (1.0 - sigma))).astype(
        jnp.bfloat16
    )
    up_grad = (hidden_grad * pre_gate * sigma).astype(jnp.bfloat16)
    first = lax.dot_general(
        gate_grad, w_gate, (((1,), (1,)), ((), ())), preferred_element_type=jnp.float32
    )
    second = lax.dot_general(
        up_grad, w_up, (((1,), (1,)), ((), ())), preferred_element_type=jnp.float32
    )
    return first + second


def per_device(activations, out_grad, routes, gates, gate_weight, up_weight, down_weight):
    experts = lax.axis_size("expert")
    tok_dev, top_k = routes.shape
    capacity = 3 * tok_dev * top_k // (2 * experts)
    pair_count = tok_dev * top_k
    flat_ids = routes.reshape(-1)
    onehot = (flat_ids[:, None] == jnp.arange(experts, dtype=jnp.int32)[None, :]).astype(jnp.int32)
    position = jnp.sum(onehot * (jnp.cumsum(onehot, axis=0) - 1), axis=1)
    dest_slot = flat_ids * capacity + position
    slot_source = (
        jnp.full((experts * capacity,), -1, jnp.int32)
        .at[dest_slot]
        .set(jnp.arange(pair_count, dtype=jnp.int32))
    )
    filled = slot_source >= 0
    source = jnp.maximum(slot_source, 0)
    row_index = source // top_k
    slot_gate = jnp.where(filled, gates.reshape(-1)[source], jnp.zeros((), jnp.float32))
    w_gate = gate_weight[0]
    w_up = up_weight[0]
    w_down = down_weight[0]
    x_full, d_full = (
        lax.all_gather(activations, "tensor", axis=1, tiled=True),
        lax.all_gather(out_grad, "tensor", axis=1, tiled=True),
    )
    x_slots = jnp.where(filled[:, None], x_full[row_index], jnp.zeros((), x_full.dtype))
    d_slots = (slot_gate[:, None] * d_full[row_index].astype(jnp.float32)).astype(jnp.bfloat16)
    x_slots, d_slots = (
        x_slots.reshape(experts, capacity, -1),
        d_slots.reshape(experts, capacity, -1),
    )
    x_recv = lax.all_to_all(x_slots, "expert", split_axis=0, concat_axis=0, tiled=True)
    block_rows = x_recv.shape[1]
    width = x_recv.shape[2]
    partial_value = expert_grads(
        x_recv.reshape(-1, width),
        lax.all_to_all(d_slots, "expert", split_axis=0, concat_axis=0, tiled=True).reshape(
            -1, width
        ),
        w_gate,
        w_up,
        w_down,
    )
    partial_value = partial_value.reshape(experts, block_rows, width).astype(jnp.bfloat16)
    returned = lax.all_to_all(partial_value, "expert", split_axis=0, concat_axis=0, tiled=True)
    slot_grad = lax.psum_scatter(
        returned.astype(jnp.float32).astype(jnp.bfloat16), "tensor", scatter_dimension=2, tiled=True
    )
    flat_back = slot_grad.reshape(experts * capacity, -1)
    picked = flat_back[dest_slot].astype(jnp.float32).reshape(tok_dev, top_k, -1)
    return jnp.sum(picked, axis=1).astype(jnp.bfloat16)


def solution(mesh):
    return jax.shard_map(
        per_device,
        mesh=mesh,
        in_specs=(
            P(("group", "expert"), "tensor"),
            P(("group", "expert"), "tensor"),
            P(("group", "expert"), None),
            P(("group", "expert"), None),
            P("expert", None, "tensor"),
            P("expert", None, "tensor"),
            P("expert", "tensor", None),
        ),
        out_specs=P(("group", "expert"), "tensor"),
        check_vma=False,
    )
```

profile of v0, /device:TPU:0, one launch (start us, length us, event | category | flops | bytes accessed | tf_op | source)
XLA Modules:
  0.0 530.9 jit_solution(6551022024097637044)
XLA Ops:
  6.5 0.0 all-gather.5.cloned.1.call-start
  6.5 0.7 all-gather.5.cloned.1.call-update
  7.3 0.8 copy.11
  8.0 0.1 eq.29
  8.2 0.1 eq.25
  8.3 1.2 reduce-window.6
  9.6 0.1 slice.16
  9.6 0.1 copy.13
  9.8 0.1 copy.14
  9.9 0.7 broadcast_multiply_fusion
  10.6 0.1 copy.10
  10.7 0.1 mul.50
  10.8 0.8 copy.15
  11.6 0.1 reshape.83
  11.8 0.1 add_bitcast_fusion
  11.9 1.4 scatter_custom_fusion
  13.3 2.8 gather_fusion
  16.1 0.1 broadcast_in_dim.37
  16.2 16.6 %all-gather.5.cloned.1.call-done = bf16[128,7168]{1,0:T(8,128)(2,1)} async-done(((bf16[128,1792]{1,0:T(8,128)(2,1)}), bf16[128,7168]{1,0:T(8,128)(2,1)}) %all-gather.5.cloned.1.call-update) | async-done | bytes 1835024 | tf_op jit(solution)/shard_map/all_gather | solution.py:49
  32.8 15.0 %gather_fusion.2 = bf16[384,7168]{1,0:T(8,128)(2,1)} fusion(bf16[128,7168]{1,0:T(8,128)(2,1)} %all-gather.5.cloned.1.call-done, s32[1024]{0:T(1024)S(1)} %pad_clamp_fusion.1), kind=kCustom, calls=%fused_computation.2 | custom fusion | bytes 11011584 | tf_op jit(solution)/shard_map/gather | solution.py:52
  47.7 5.4 %broadcast_select_fusion = bf16[4,96,7168]{2,1,0:T(8,128)(2,1)} fusion(bf16[4,96,7168]{2,1,0:T(8,128)(2,1)} %bitcast.52, pred[4,96]{1,0:T(4,128)(4,1)S(1)} %broadcast_in_dim.37), kind=kLoop, calls=%fused_computation.17 | loop fusion | flops 2752512 | bytes 11010432 | tf_op jit(solution)/shard_map/jit(_where)/select_n | solution.py:52
  53.2 5.1 all-to-all-start.1
  58.3 0.2 all-gather.3.cloned.1.call-start
  58.5 0.5 all-gather.3.cloned.1.call-update
  59.0 0.1 mul.52
  59.1 23.2 %all-gather.3.cloned.1.call-done = bf16[128,7168]{1,0:T(8,128)(2,1)} async-done(((bf16[128,1792]{1,0:T(8,128)(2,1)}), bf16[128,7168]{1,0:T(8,128)(2,1)}) %all-gather.3.cloned.1.call-update) | async-done | bytes 1835024 | tf_op jit(solution)/shard_map/all_gather | solution.py:50
  82.3 15.0 %gather_fusion.1 = bf16[384,7168]{1,0:T(8,128)(2,1)} fusion(bf16[128,7168]{1,0:T(8,128)(2,1)} %all-gather.3.cloned.1.call-done, s32[1024]{0:T(1024)S(1)} %pad_clamp_fusion.1), kind=kCustom, calls=%fused_computation.1 | custom fusion | bytes 11011584 | tf_op jit(solution)/shard_map/gather | solution.py:53
  97.3 6.6 %fusion = bf16[4,96,7168]{2,1,0:T(8,128)(2,1)} fusion(bf16[4,96,7168]{2,1,0:T(8,128)(2,1)} %bitcast.51, f32[4,96]{1,0:T(4,128)S(1)} %mul.52), kind=kLoop, calls=%fused_computation.6 | loop fusion | flops 8257536 | bytes 11011584 | tf_op jit(solution)/shard_map/convert_element_type | solution.py:53
  103.9 76.4 %all-to-all-done.1 = bf16[4,96,7168]{2,1,0:T(8,128)(2,1)} async-done(((bf16[4,96,7168]{2,1,0:T(8,128)(2,1)}), bf16[4,96,7168]{2,1,0:T(8,128)(2,1)}, u32[]{:S(2)}, u32[]{:S(2)}) %all-to-all-start.1) | async-done | bytes 5505056 | tf_op jit(solution)/shard_map/all_to_all | solution.py:58
  180.2 5.1 all-to-all-start
  185.4 0.3 reduce-scatter.2.cloned.1.call-start
  185.7 7.0 %fusion.3 = f32[384,512]{1,0:T(8,128)S(1)} fusion(bf16[384,7168]{1,0:T(8,128)(2,1)} %bitcast.8, bf16[1,7168,512]{2,1,0:T(8,128)(2,1)} %param.11), kind=kOutput, calls=%fused_computation.10 | convolution fusion | flops 2818572288 | bytes 13631488 | tf_op jit(solution)/shard_map/dot_general | solution.py:8
  192.6 113.9 %all-to-all-done = bf16[4,96,7168]{2,1,0:T(8,128)(2,1)} async-done(((bf16[4,96,7168]{2,1,0:T(8,128)(2,1)}), bf16[4,96,7168]{2,1,0:T(8,128)(2,1)}, u32[]{:S(2)}, u32[]{:S(2)}) %all-to-all-start) | async-done | bytes 5505056 | tf_op jit(solution)/shard_map/all_to_all | solution.py:63
  306.5 0.0 slice-start
  306.6 7.1 %fusion.8 = f32[384,512]{1,0:T(8,128)S(1)} fusion(bf16[384,7168]{1,0:T(8,128)(2,1)} %bitcast.5, bf16[1,512,7168]{2,1,0:T(8,128)(2,1)} %param.13), kind=kOutput, calls=%fused_computation.15 | convolution fusion | flops 2818572288 | bytes 13631488 | tf_op jit(solution)/shard_map/dot_general | solution.py:10
  313.7 0.0 slice-start.1
  313.7 8.0 %fusion.19 = bf16[384,512]{1,0:T(8,128)(2,1)S(1)} fusion(f32[384,512]{1,0:T(8,128)S(1)} %fusion.8, bf16[384,7168]{1,0:T(8,128)(2,1)} %bitcast.8, bf16[1,7168,512]{2,1,0:T(8,128)(2,1)} %param.12, f32[384,512]{1,0:T(8,128)S(1)} %fusion.3), kind=kOutput, calls=%fused_computation.21 | convolution fusion | flops 2820538368 | bytes 14811136 | tf_op jit(solution)/shard_map/dot_general | solution.py:9
  321.7 0.0 slice-done
  321.7 0.0 slice-done.1
  321.8 5.8 %fusion.1 = f32[384,7168]{1,0:T(8,128)} fusion(bf16[384,512]{1,0:T(8,128)(2,1)S(1)} %fusion.19, bf16[1,7168,512]{2,1,0:T(8,128)(2,1)S(1)} %bitcast.54), kind=kOutput, calls=%fused_computation.8 | convolution fusion | flops 2818572288 | bytes 18743296 | tf_op jit(solution)/shard_map/dot_general | solution.py:18
  327.5 11.3 %add_convert_fusion = bf16[384,7168]{1,0:T(8,128)(2,1)} fusion(f32[384,7168]{1,0:T(8,128)} %fusion.1, bf16[1,7168,512]{2,1,0:T(8,128)(2,1)} %param.12, f32[384,512]{1,0:T(8,128)S(1)} %fusion.8, f32[384,512]{1,0:T(8,128)S(1)} %fusion.3), kind=kOutput, calls=%fused_computation.7 | convolution fusion | flops 2825256960 | bytes 25427968 | tf_op jit(solution)/shard_map/dot_general | solution.py:21
  338.9 127.0 %all_to_all.15 = bf16[4,96,7168]{2,1,0:T(8,128)(2,1)} all-to-all(bf16[4,96,7168]{2,1,0:T(8,128)(2,1)} %bitcast.50), channel_id=1, replica_groups=mesh['group'=2,'expert'=4,'tensor'=4] {'expert'}, dimensions={0} | all-to-all | bytes 11010048 | tf_op jit(solution)/shard_map/all_to_all | solution.py:71
  465.9 0.0 reduce-scatter.2.cloned.1.call-update
  465.9 51.2 %reduce-scatter.2.cloned.1.call-done = bf16[4,96,1792]{2,1,0:T(8,128)(2,1)} async-done(((bf16[4,96,7168]{2,1,0:T(8,128)(2,1)}), bf16[4,96,1792]{2,1,0:T(8,128)(2,1)}) %reduce-scatter.2.cloned.1.call-update) | async-done | bytes 1376272 | tf_op jit(solution)/shard_map/reduce_scatter | solution.py:72
  517.1 3.7 gather_fusion.3
  520.8 0.3 gather.21
  521.2 3.2 reduce_sum.25
  (12 shorter events, 0.1 us)
Async XLA Ops:
  6.5 26.2 %all-gather.5.cloned.1.call-start = ((), (), s32[]{:S(2)}) async-start(), calls=%async_computation.5 | async-start | bytes 2293760 | tf_op jit(solution)/shard_map/all_gather | solution.py:49
  53.2 127.1 %all-to-all-start.1 = ((bf16[4,96,7168]{2,1,0:T(8,128)(2,1)}), bf16[4,96,7168]{2,1,0:T(8,128)(2,1)}, u32[]{:S(2)}, u32[]{:S(2)}) async-start(bf16[4,96,7168]{2,1,0:T(8,128)(2,1)} %broadcast_select_fusion), calls=%async_computation.1 | async-start | bytes 11010048 | tf_op jit(solution)/shard_map/all_to_all | solution.py:58
  58.3 24.0 %all-gather.3.cloned.1.call-start = ((), (), s32[]{:S(2)}) async-start(), calls=%async_computation.4 | async-start | bytes 2293760 | tf_op jit(solution)/shard_map/all_gather | solution.py:50
  180.2 126.3 %all-to-all-start = ((bf16[4,96,7168]{2,1,0:T(8,128)(2,1)}), bf16[4,96,7168]{2,1,0:T(8,128)(2,1)}, u32[]{:S(2)}, u32[]{:S(2)}) async-start(bf16[4,96,7168]{2,1,0:T(8,128)(2,1)} %fusion), calls=%async_computation | async-start | bytes 11010048 | tf_op jit(solution)/shard_map/all_to_all | solution.py:63
  185.4 331.7 %reduce-scatter.2.cloned.1.call-start = ((), (), s32[]{:S(2)}) async-start(), calls=%async_computation.6 | async-start | bytes 6881280 | tf_op jit(solution)/shard_map/reduce_scatter | solution.py:72
  306.5 15.2 %slice-start = ((s8[7340032]{0:T(1024)(128)(4,1)}), s8[4194304]{0:T(1024)(128)(4,1)S(1)}, s32[]{:S(2)}) async-start(s8[7340032]{0:T(1024)(128)(4,1)} %bitcast.53), calls=%async_computation.7 | async-start | bytes 8388608
  313.7 8.0 %slice-start.1 = ((s8[7340032]{0:T(1024)(128)(4,1)}), s8[3145728]{0:T(1024)(128)(4,1)S(1)}, s32[]{:S(2)}) async-start(s8[7340032]{0:T(1024)(128)(4,1)} %bitcast.53), calls=%async_computation.8 | async-start | bytes 6291456
Sparse Core Ops, SparseCore 0:
  8.9 23.8 all-gather.4
  60.7 21.5 all-gather.2
  466.1 51.0 reduce-scatter.1
where the time goes:
time: 531 us
  waiting for transfers between devices  282 us (53%)
  blocking collectives  127 us (24%)
  local copies, waits for them, and re-layouts  40.8 us (8%)
  matrix products  39.2 us (7%)
  other arithmetic  17.4 us (3%)
  between operations  13.3 us (3%)
  starting transfers between devices  10.7 us (2%)
    all_to_all x1, blocking collectives, per_device(): lax.all_to_all(partial_value, 'expert', split_axis=0, concat_axis=0, tile...  127 us
    all_to_all x1, waiting for transfers between devices, per_device(): lax.all_to_all(d_slots, 'expert', split_axis=0, concat_axis=0, tiled=True)  114 us
    all_to_all x1, waiting for transfers between devices, per_device(): lax.all_to_all(x_slots, 'expert', split_axis=0, concat_axis=0, tiled=True)  76.4 us
    reduce_scatter x1, waiting for transfers between devices, per_device(): lax.psum_scatter(returned.astype(jnp.float32).astype(jnp.bfloat16), 'tens...  51.2 us
    all_gather x1, waiting for transfers between devices, per_device(): lax.all_gather(out_grad, 'tensor', axis=1, tiled=True)  23.2 us
    all_gather x1, waiting for transfers between devices, per_device(): lax.all_gather(activations, 'tensor', axis=1, tiled=True)  16.6 us
    gather x1, local copies, waits for them, and re-layouts, per_device(): d_full[row_index].astype(jnp.float32)  15 us
    gather x1, local copies, waits for them, and re-layouts, per_device(): x_full[row_index]  15 us
  transfers between devices with their start and end apart: 5, of which 5 were waited for; matrix products, arithmetic and copies ran while one was open for 7% of the time, Pallas kernels for 0%

commit v1 on v0

v1 whole, which is shorter than its diff:
```python
import functools

import jax
import jax.numpy as jnp
from jax import lax
from jax.experimental import pallas as pl
from jax.experimental.pallas import tpu as pltpu
from jax.sharding import PartitionSpec as P

MESH = pl.DeviceIdType.MESH
F32 = jnp.float32
BF16 = jnp.bfloat16
NT = (((1,), (1,)), ((), ()))


def flip(a, k, n):
    out, bit = 0, 1
    while bit < n:
        out = out + bit * lax.rem(lax.div(a, bit) + lax.div(k, bit), 2)
        bit *= 2
    return out


def kernel(
    E, T, cap,
    x_ref, d_ref, routes_ref, gates_ref, wg_hbm, wu_hbm, wd_hbm, out_ref,
    wg, wu, wd, xd_send, xd, pt, pre_g, pre_u, hid, gg, ug, own,
    a_send, a_recv, b_send, b_recv, c_send, c_recv,
    w_sem, zs, zr, xs, xr, cs, cr, as_, ar, bs, br, rs, rr,
):
    X = T // 2
    W = x_ref.shape[1]
    tok = x_ref.shape[0]
    me = lax.axis_index("expert")
    mt = lax.axis_index("tensor")
    mx, mc = lax.div(mt, 2), lax.rem(mt, 2)
    oc = 1 - mc
    partner = mx * 2 + oc

    loads = [
        pltpu.make_async_copy(h, v, w_sem.at[i])
        for i, (h, v) in enumerate(((wg_hbm, wg), (wu_hbm, wu), (wd_hbm, wd)))
    ]
    for c in loads:
        c.start()

    barrier = pltpu.get_barrier_semaphore()

    def greet_z(k, _):
        pl.semaphore_signal(barrier, inc=1, device_id={"expert": lax.rem(me + k, E)}, device_id_type=MESH)
        return 0

    lax.fori_loop(1, E, greet_z, 0)
    for j in range(1, X):
        pl.semaphore_signal(
            barrier, inc=1, device_id={"tensor": lax.rem(mx + j, X) * 2 + mc}, device_id_type=MESH
        )
    pl.semaphore_signal(barrier, inc=1, device_id={"tensor": partner}, device_id_type=MESH)

    lanes = pt.shape[2]
    expert_lane = lax.broadcasted_iota(jnp.int32, (tok, 128), 1)
    first, second = routes_ref[:, 0:1], routes_ref[:, 1:2]
    on_first, on_second = first == expert_lane, second == expert_lane
    named = jnp.where(on_first | on_second, 1.0, 0.0).astype(F32)
    weight = jnp.where(on_first, gates_ref[:, 0:1], 0.0) + jnp.where(on_second, gates_ref[:, 1:2], 0.0)
    row = lax.broadcasted_iota(jnp.int32, (tok, tok), 0)
    col = lax.broadcasted_iota(jnp.int32, (tok, tok), 1)
    before = jnp.where(col < row, 1.0, 0.0).astype(BF16)
    rank = jnp.dot(before, named.astype(BF16), preferred_element_type=F32)
    place = jnp.where(named > 0, rank, -1.0)
    slot_lane = lax.broadcasted_iota(jnp.int32, (tok, lanes), 1).astype(F32)

    def z_copy(e):
        return pltpu.make_async_remote_copy(
            src_ref=xd_send.at[e], dst_ref=xd.at[mt, me], send_sem=zs.at[e], recv_sem=zr.at[me],
            device_id={"expert": e}, device_id_type=MESH,
        )

    def z_arrival(s):
        return pltpu.make_async_remote_copy(
            src_ref=xd_send.at[s], dst_ref=xd.at[mt, s], send_sem=zs.at[s], recv_sem=zr.at[s],
            device_id={"expert": s}, device_id_type=MESH,
        )

    def fill(e, dst):
        chosen = expert_lane == e
        at = jnp.sum(jnp.where(chosen, place, 0.0), axis=1, keepdims=True)
        g = jnp.sum(jnp.where(chosen, weight, 0.0), axis=1, keepdims=True)
        sel = jnp.where(at == slot_lane, 1.0, 0.0).astype(F32)
        pt[e] = sel.astype(BF16)
        sel_t = sel.T[:cap]
        slot_gate = jnp.sum((sel * g).T[:cap], axis=1, keepdims=True)
        pick = sel_t.astype(BF16)
        dst[0:cap, :] = jnp.dot(pick, x_ref[...], preferred_element_type=F32).astype(BF16)
        d_rows = jnp.dot(pick, d_ref[...], preferred_element_type=F32)
        dst[cap : 2 * cap, :] = (slot_gate * d_rows).astype(BF16)

    def x_copy(s, j):
        return pltpu.make_async_remote_copy(
            src_ref=xd.at[mt, s], dst_ref=xd.at[mt, s],
            send_sem=xs.at[j, s], recv_sem=xr.at[j, s],
            device_id={"tensor": lax.rem(mx + j, X) * 2 + mc}, device_id_type=MESH,
        )

    def x_arrival(s, j):
        src = lax.rem(mx - j + X, X) * 2 + mc
        return pltpu.make_async_remote_copy(
            src_ref=xd.at[src, s], dst_ref=xd.at[src, s],
            send_sem=xs.at[j, s], recv_sem=xr.at[j, s],
            device_id={"tensor": src}, device_id_type=MESH,
        )

    def core_copy(s, xi):
        t = xi * 2 + mc
        return pltpu.make_async_remote_copy(
            src_ref=xd.at[t, s], dst_ref=xd.at[t, s], send_sem=cs.at[xi, s], recv_sem=cr.at[xi, s],
            device_id={"tensor": partner}, device_id_type=MESH,
        )

    def core_arrival(s, xi):
        t = xi * 2 + oc
        return pltpu.make_async_remote_copy(
            src_ref=xd.at[t, s], dst_ref=xd.at[t, s], send_sem=cs.at[xi, s], recv_sem=cr.at[xi, s],
            device_id={"tensor": partner}, device_id_type=MESH,
        )

    def spread(s):
        for j in range(1, X):
            x_copy(s, j).start()
        core_copy(s, mx).start()

    def a_copy(s, xi):
        return pltpu.make_async_remote_copy(
            src_ref=a_send.at[s, xi], dst_ref=a_recv.at[s, xi],
            send_sem=as_.at[xi, s], recv_sem=ar.at[xi, s],
            device_id={"tensor": partner}, device_id_type=MESH,
        )

    def b_copy(s, j):
        return pltpu.make_async_remote_copy(
            src_ref=b_send.at[s, j], dst_ref=b_recv.at[s, j],
            send_sem=bs.at[j, s], recv_sem=br.at[j, s],
            device_id={"tensor": lax.rem(mx + j, X) * 2 + mc}, device_id_type=MESH,
        )

    def c_copy(s):
        return pltpu.make_async_remote_copy(
            src_ref=c_send.at[s], dst_ref=c_recv.at[me], send_sem=rs.at[s], recv_sem=rr.at[me],
            device_id={"expert": s}, device_id_type=MESH,
        )

    def c_arrival(s):
        return pltpu.make_async_remote_copy(
            src_ref=c_send.at[s], dst_ref=c_recv.at[s], send_sem=rs.at[s], recv_sem=rr.at[s],
            device_id={"expert": s}, device_id_type=MESH,
        )

    fill(me, xd.at[mt, me])
    pl.semaphore_wait(barrier, (E - 1) + (X - 1) + 1)
    spread(me)

    def send_z(k, _):
        e = flip(me, k, E)
        fill(e, xd_send.at[e])
        z_copy(e).start()
        return 0

    lax.fori_loop(1, E, send_z, 0)
    for c in loads:
        c.wait()

    def forward(s, t):
        wide = pl.ds(pl.multiple_of(t * W, W), W)
        x_rows = xd[t, s, 0:cap, :]
        d_rows = xd[t, s, cap : 2 * cap, :]
        pre_g[...] += jnp.dot(x_rows, wg[wide, :], preferred_element_type=F32)
        pre_u[...] += jnp.dot(x_rows, wu[wide, :], preferred_element_type=F32)
        hid[...] += lax.dot_general(d_rows, wd[:, wide], NT, preferred_element_type=F32)

    def part_of(t):
        wide = pl.ds(pl.multiple_of(t * W, W), W)
        return lax.dot_general(gg[...], wg[wide, :], NT, preferred_element_type=F32) + lax.dot_general(
            ug[...], wu[wide, :], NT, preferred_element_type=F32
        )

    def finish(s):
        total = own[s]
        for j in range(1, X):
            b_copy(s, j).wait_recv()
            total = total + b_recv[s, j].astype(F32)
        c_send[s] = total.astype(BF16)

        @pl.when(s != me)
        def _():
            c_copy(s).start()

    def chunk(k, _):
        s = flip(me, k, E)

        @pl.when(k + 1 < E)
        def _():
            ahead = flip(me, k + 1, E)
            z_arrival(ahead).wait_recv()
            spread(ahead)

        pre_g[...] = jnp.zeros_like(pre_g)
        pre_u[...] = jnp.zeros_like(pre_u)
        hid[...] = jnp.zeros_like(hid)

        def slice_step(i, _):
            @pl.when(i == 1)
            def _():
                core_arrival(s, mx).wait_recv()

            for j in range(1, X):
                src = lax.rem(mx - j + X, X)

                @pl.when(i == 1 + j)
                def _():
                    x_arrival(s, j).wait_recv()
                    core_copy(s, src).start()

                @pl.when(i == X + j)
                def _():
                    core_arrival(s, src).wait_recv()

            j = jnp.where(i < 2, 0, jnp.where(i <= X, i - 1, i - X))
            other = jnp.where(i < 2, i, jnp.where(i <= X, 0, 1))
            xi = lax.rem(mx - j + X, X)
            core = lax.rem(mc + other, 2)
            forward(s, xi * 2 + core)
            return 0

        lax.fori_loop(0, T, slice_step, 0)

        pg, pu, hg = pre_g[...], pre_u[...], hid[...]
        sigma = jax.nn.sigmoid(pg)
        gg[...] = (hg * pu * sigma * (1.0 + pg * (1.0 - sigma))).astype(BF16)
        ug[...] = (hg * pg * sigma).astype(BF16)

        def give(i, _):
            xi = lax.rem(mx + 1 + i, X)
            a_send[s, xi] = part_of(xi * 2 + oc).astype(BF16)
            a_copy(s, xi).start()
            return 0

        lax.fori_loop(0, X, give, 0)

        def keep(j, _):
            xi = lax.rem(mx + j, X)
            mine = part_of(xi * 2 + mc)
            a_copy(s, xi).wait_recv()
            b_send[s, j] = (mine + a_recv[s, xi].astype(F32)).astype(BF16)
            b_copy(s, j).start()
            return 0

        lax.fori_loop(1, X, keep, 0)
        mine = part_of(mx * 2 + mc)
        a_copy(s, mx).wait_recv()
        own[s] = mine + a_recv[s, mx].astype(F32)

        @pl.when(k >= 1)
        def _():
            finish(flip(me, k - 1, E))

        return 0

    lax.fori_loop(0, E, chunk, 0)
    finish(flip(me, E - 1, E))

    def add(s, _):
        @pl.when(s != me)
        def _():
            c_arrival(s).wait_recv()

        return 0

    lax.fori_loop(0, E, add, 0)
    total = jnp.dot(pt[me, :, :cap], c_send[me], preferred_element_type=F32)
    for k in range(1, E):
        s = flip(me, k, E)
        total = total + jnp.dot(pt[s, :, :cap], c_recv[s], preferred_element_type=F32)
    out_ref[...] = total.astype(BF16)

    def drain(s, _):
        @pl.when(s != me)
        def _():
            z_copy(s).wait_send()
            c_copy(s).wait_send()

        for j in range(1, X):
            x_copy(s, j).wait_send()
            b_copy(s, j).wait_send()
        for xi in range(X):
            core_copy(s, xi).wait_send()
            a_copy(s, xi).wait_send()
        return 0

    lax.fori_loop(0, E, drain, 0)


def per_device(activations, out_grad, routes, gates, gate_weight, up_weight, down_weight):
    E = lax.axis_size("expert")
    T = lax.axis_size("tensor")
    X = T // 2
    tok, top = routes.shape
    W = activations.shape[1]
    D, FF = gate_weight.shape[1:]
    need = 3 * tok * top // (2 * E)
    cap = -(-need // 16) * 16
    wide = -(-cap // 128) * 128
    vmem = pl.BlockSpec(memory_space=pltpu.VMEM)
    anywhere = pl.BlockSpec(memory_space=pl.ANY)
    dma = pltpu.SemaphoreType.DMA
    return pl.pallas_call(
        functools.partial(kernel, E, T, cap),
        out_shape=jax.ShapeDtypeStruct((tok, W), BF16),
        in_specs=[vmem] * 4 + [anywhere] * 3,
        out_specs=vmem,
        scratch_shapes=[
            pltpu.VMEM((D, FF), BF16),
            pltpu.VMEM((D, FF), BF16),
            pltpu.VMEM((FF, D), BF16),
            pltpu.VMEM((E, 2 * cap, W), BF16),
            pltpu.VMEM((T, E, 2 * cap, W), BF16),
            pltpu.VMEM((E, tok, wide), BF16),
            pltpu.VMEM((cap, FF), F32),
            pltpu.VMEM((cap, FF), F32),
            pltpu.VMEM((cap, FF), F32),
            pltpu.VMEM((cap, FF), BF16),
            pltpu.VMEM((cap, FF), BF16),
            pltpu.VMEM((E, cap, W), F32),
            pltpu.VMEM((E, X, cap, W), BF16),
            pltpu.VMEM((E, X, cap, W), BF16),
            pltpu.VMEM((E, X, cap, W), BF16),
            pltpu.VMEM((E, X, cap, W), BF16),
            pltpu.VMEM((E, cap, W), BF16),
            pltpu.VMEM((E, cap, W), BF16),
            dma((3,)),
            dma((E,)), dma((E,)),
            dma((X, E)), dma((X, E)),
            dma((X, E)), dma((X, E)),
            dma((X, E)), dma((X, E)),
            dma((X, E)), dma((X, E)),
            dma((E,)), dma((E,)),
        ],
        compiler_params=pltpu.CompilerParams(
            collective_id=0, has_side_effects=True, vmem_limit_bytes=62 * 1024 * 1024
        ),
        cost_estimate=pl.CostEstimate(
            flops=10 * E * cap * D * FF, bytes_accessed=6 * D * FF, transcendentals=E * cap * FF
        ),
    )(activations, out_grad, routes, gates, gate_weight[0], up_weight[0], down_weight[0])


def solution(mesh):
    return jax.shard_map(
        per_device,
        mesh=mesh,
        in_specs=(
            P(("group", "expert"), "tensor"),
            P(("group", "expert"), "tensor"),
            P(("group", "expert"), None),
            P(("group", "expert"), None),
            P("expert", None, "tensor"),
            P("expert", None, "tensor"),
            P("expert", "tensor", None),
        ),
        out_specs=P(("group", "expert"), "tensor"),
        check_vma=False,
    )
```

time: 531 us -> 132 us (0.25)
  waiting for transfers between devices: 282 us -> 0 us
  Pallas kernels: 0 us -> 127 us
  blocking collectives: 127 us -> 0 us
  matrix products: 39.2 us -> 0 us
  local copies, waits for them, and re-layouts: 40.8 us -> 4.63 us
  other arithmetic: 17.4 us -> 0 us
  between operations: 13.3 us -> 0.01 us
  starting transfers between devices: 10.7 us -> 0 us
    all_to_all x2 -> x0, waiting for transfers between devices: 190 us -> none  [the longest x1 114 us: per_device(): lax.all_to_all(d_slots, 'expert', split_axis=0, concat_axis=0, tiled=True)]
    pallas_call x0 -> x1, Pallas kernels: none -> 127 us  [per_device(): pl.pallas_call(functools.partial(kernel, E, T, cap), out_shape=jax.ShapeD...]
    all_to_all x1 -> x0, blocking collectives: 127 us -> none  [per_device(): lax.all_to_all(partial_value, 'expert', split_axis=0, concat_axis=0, tile...]
    reduce_scatter x1 -> x0, waiting for transfers between devices: 51.2 us -> none  [per_device(): lax.psum_scatter(returned.astype(jnp.float32).astype(jnp.bfloat16), 'tens...]
    all_gather x2 -> x0, waiting for transfers between devices: 39.7 us -> none  [the longest x1 23.2 us: per_device(): lax.all_gather(out_grad, 'tensor', axis=1, tiled=True)]
    dot_general x5 -> x0, matrix products: 39.2 us -> none  [the longest x1 11.3 us: expert_grads(): lax.dot_general(up_grad, w_up, (((1,), (1,)), ((), ())), preferred_elemen...]
    gather x5 -> x0, local copies, waits for them, and re-layouts: 36.7 us -> none  [the longest x1 15 us: per_device(): d_full[row_index].astype(jnp.float32)]
    all_to_all x2 -> x0, starting transfers between devices: 10.2 us -> none  [the longest x1 5.14 us: per_device(): lax.all_to_all(d_slots, 'expert', split_axis=0, concat_axis=0, tiled=True)]
  transfers between devices with their start and end apart: 5 -> 0, of which waited for: 5 -> 0; matrix products, arithmetic and copies ran while one was open for 7% -> 0% of each run, Pallas kernels for 0% -> 0%
where the time goes in v1:
time: 132 us
  Pallas kernels  127 us (96%)
  local copies, waits for them, and re-layouts  4.63 us (4%)
    pallas_call x1, Pallas kernels, per_device(): pl.pallas_call(functools.partial(kernel, E, T, cap), out_shape=jax.ShapeD...  127 us
    unnamed x3, local copies, waits for them, and re-layouts  4.63 us

profile of v1, /device:TPU:0, one launch (start us, length us, event | category | flops | bytes accessed | tf_op | source)
XLA Modules:
  0.0 131.7 jit_solution(6146055557676030631)
XLA Ops:
  0.0 1.4 %copy.8.routes_ref = s32[128,2]{1,0:T(8,128)} copy(s32[128,2]{0,1:T(2,128)} %param.9) | data formatting | bytes 2048 | tf_op args[2]
  1.4 1.4 %copy.9.gates_ref = f32[128,2]{1,0:T(8,128)} copy(f32[128,2]{0,1:T(2,128)} %param.10) | data formatting | bytes 2048 | tf_op args[3]
  2.8 127.1 %shard_map.73 = bf16[128,1792]{1,0:T(8,128)(2,1)} custom-call(bf16[128,1792]{1,0:T(8,128)(2,1)} %x_ref.1, bf16[128,1792]{1,0:T(8,128)(2,1)} %d_ref.1, s32[128,2]{1,0:T(8,128)} %copy.8.routes_ref, f32[128,2]{1,0:T(8,128)} %copy.9.gates_ref, bf16[7168,512]{1,0:T(8,128)(2,1)} %bitcast.3, bf16[7168,512]{1,0:T(8,128)(2,1)} %bitcast.4, bf16[512,7168]{1,0:T(8,128)(2,1)} %bitcast.5), custom_call_target="tpu_custom_call" | custom-call | flops 14092861440 | bytes 22020096 | tf_op jit(solution)/shard_map/pallas_call | solution.py:315
  129.9 1.8 %copy.11 = bf16[128,1792]{1,0:T(8,128)(2,1)} copy(bf16[128,1792]{1,0:T(8,128)(2,1)} %shard_map.73) | data formatting | bytes 917504

commit v2 on v1

v2 whole, which is shorter than its diff:
```python
import functools

import jax
import jax.numpy as jnp
from jax import lax
from jax.experimental import pallas as pl
from jax.experimental.pallas import tpu as pltpu
from jax.sharding import PartitionSpec as P

MESH = pl.DeviceIdType.MESH
F32 = jnp.float32
BF16 = jnp.bfloat16
NT = (((1,), (1,)), ((), ()))
TN = (((0,), (0,)), ((), ()))


def nth(z, k, n):
    low = z < n // 2
    edge = jnp.where(low, z, n - 1 - z)
    step = jnp.where(low, -1, 1)
    odd = lax.rem(k, 2)
    near = jnp.where(odd == 1, step * lax.div(k + 1, 2), -step * lax.div(k, 2))
    return z + jnp.where(k <= 2 * edge, near, -step * (k - edge))


def kernel(
    E, T, cap,
    x_ref, d_ref, routes_ref, gates_ref, wg_hbm, wu_hbm, wd_hbm, out_ref,
    wg, wu, wd, xd_send, xd, pt, pre_g, pre_u, hid, gg, ug, own,
    a_send, a_recv, b_send, b_recv, c_send, c_recv,
    w_sem, zs, zr, xs, xr, cs, cr, as_, ar, bs, br, rs, rr,
):
    X = T // 2
    W = x_ref.shape[1]
    tok = x_ref.shape[0]
    me = lax.axis_index("expert")
    mt = lax.axis_index("tensor")
    mx, mc = lax.div(mt, 2), lax.rem(mt, 2)
    oc = 1 - mc
    partner = mx * 2 + oc

    loads = [
        pltpu.make_async_copy(h, v, w_sem.at[i])
        for i, (h, v) in enumerate(((wg_hbm, wg), (wu_hbm, wu), (wd_hbm, wd)))
    ]
    for c in loads:
        c.start()

    barrier = pltpu.get_barrier_semaphore()

    def greet_z(k, _):
        pl.semaphore_signal(barrier, inc=1, device_id={"expert": lax.rem(me + k, E)}, device_id_type=MESH)
        return 0

    lax.fori_loop(1, E, greet_z, 0)
    for j in range(1, X):
        pl.semaphore_signal(
            barrier, inc=1, device_id={"tensor": lax.rem(mx + j, X) * 2 + mc}, device_id_type=MESH
        )
    pl.semaphore_signal(barrier, inc=1, device_id={"tensor": partner}, device_id_type=MESH)

    deep = -(-E // 16) * 16
    expert_row = lax.broadcasted_iota(jnp.int32, (deep, tok), 0)
    on_first, on_second = routes_ref[0:1, :] == expert_row, routes_ref[1:2, :] == expert_row
    named = jnp.where(on_first | on_second, 1.0, 0.0).astype(F32)
    weight = jnp.where(on_first, gates_ref[0:1, :], 0.0) + jnp.where(on_second, gates_ref[1:2, :], 0.0)
    row = lax.broadcasted_iota(jnp.int32, (tok, tok), 0)
    col = lax.broadcasted_iota(jnp.int32, (tok, tok), 1)
    earlier = jnp.where(row < col, 1.0, 0.0).astype(BF16)
    rank = jnp.dot(named.astype(BF16), earlier, preferred_element_type=F32)
    place = jnp.where(named > 0, rank, -1.0)
    slot_row = lax.broadcasted_iota(jnp.int32, (cap, tok), 0).astype(F32)

    def z_copy(e, h):
        return pltpu.make_async_remote_copy(
            src_ref=xd_send.at[e, h], dst_ref=xd.at[mt, me, h], send_sem=zs.at[h, e], recv_sem=zr.at[h, me],
            device_id={"expert": e}, device_id_type=MESH,
        )

    def z_arrival(s, h):
        return pltpu.make_async_remote_copy(
            src_ref=xd_send.at[s, h], dst_ref=xd.at[mt, s, h], send_sem=zs.at[h, s], recv_sem=zr.at[h, s],
            device_id={"expert": s}, device_id_type=MESH,
        )

    def fill(e, dst):
        chosen = expert_row == e
        at = jnp.sum(jnp.where(chosen, place, 0.0), axis=0, keepdims=True)
        g = jnp.sum(jnp.where(chosen, weight, 0.0), axis=0, keepdims=True)
        sel = jnp.where(at == slot_row, 1.0, 0.0).astype(F32)
        slot_gate = jnp.sum(sel * g, axis=1, keepdims=True)
        pick = sel.astype(BF16)
        pt[e] = pick
        dst[0] = jnp.dot(pick, x_ref[...], preferred_element_type=F32).astype(BF16)
        d_rows = jnp.dot(pick, d_ref[...], preferred_element_type=F32)
        dst[1] = (slot_gate * d_rows).astype(BF16)

    def x_copy(s, h, j):
        return pltpu.make_async_remote_copy(
            src_ref=xd.at[mt, s, h], dst_ref=xd.at[mt, s, h],
            send_sem=xs.at[h, j, s], recv_sem=xr.at[h, j, s],
            device_id={"tensor": lax.rem(mx + j, X) * 2 + mc}, device_id_type=MESH,
        )

    def x_arrival(s, h, j):
        src = lax.rem(mx - j + X, X) * 2 + mc
        return pltpu.make_async_remote_copy(
            src_ref=xd.at[src, s, h], dst_ref=xd.at[src, s, h],
            send_sem=xs.at[h, j, s], recv_sem=xr.at[h, j, s],
            device_id={"tensor": src}, device_id_type=MESH,
        )

    def core_copy(s, h, xi):
        t = xi * 2 + mc
        return pltpu.make_async_remote_copy(
            src_ref=xd.at[t, s, h], dst_ref=xd.at[t, s, h],
            send_sem=cs.at[h, xi, s], recv_sem=cr.at[h, xi, s],
            device_id={"tensor": partner}, device_id_type=MESH,
        )

    def core_arrival(s, h, xi):
        t = xi * 2 + oc
        return pltpu.make_async_remote_copy(
            src_ref=xd.at[t, s, h], dst_ref=xd.at[t, s, h],
            send_sem=cs.at[h, xi, s], recv_sem=cr.at[h, xi, s],
            device_id={"tensor": partner}, device_id_type=MESH,
        )

    def spread(s, h):
        for j in range(1, X):
            x_copy(s, h, j).start()
        core_copy(s, h, mx).start()

    def a_copy(s, xi):
        return pltpu.make_async_remote_copy(
            src_ref=a_send.at[s, xi], dst_ref=a_recv.at[s, xi],
            send_sem=as_.at[xi, s], recv_sem=ar.at[xi, s],
            device_id={"tensor": partner}, device_id_type=MESH,
        )

    half = cap // 2

    def b_copy(s, j, h):
        rows = pl.ds(h * half, half)
        return pltpu.make_async_remote_copy(
            src_ref=b_send.at[s, j, rows], dst_ref=b_recv.at[s, j, rows],
            send_sem=bs.at[h, j, s], recv_sem=br.at[h, j, s],
            device_id={"tensor": lax.rem(mx + j, X) * 2 + mc}, device_id_type=MESH,
        )

    def c_copy(s, h):
        rows = pl.ds(h * half, half)
        return pltpu.make_async_remote_copy(
            src_ref=c_send.at[s, rows], dst_ref=c_recv.at[me, rows],
            send_sem=rs.at[h, s], recv_sem=rr.at[h, me],
            device_id={"expert": s}, device_id_type=MESH,
        )

    def c_arrival(s, h):
        rows = pl.ds(h * half, half)
        return pltpu.make_async_remote_copy(
            src_ref=c_send.at[s, rows], dst_ref=c_recv.at[s, rows],
            send_sem=rs.at[h, s], recv_sem=rr.at[h, s],
            device_id={"expert": s}, device_id_type=MESH,
        )

    fill(me, xd.at[mt, me])
    pl.semaphore_wait(barrier, (E - 1) + (X - 1) + 1)
    for h in range(2):
        spread(me, h)

    ahead_of = jnp.where((me == 0) | (me == E - 1), 1, 2)

    def send_z(k, _):
        e = nth(me, k, E)
        fill(e, xd_send.at[e])

        @pl.when(k <= ahead_of)
        def _():
            for h in range(2):
                z_copy(e, h).start()

        return 0

    lax.fori_loop(1, E, send_z, 0)
    for c in loads:
        c.wait()

    def forward(s, h, t):
        wide = pl.ds(pl.multiple_of(t * W, W), W)
        rows = xd[t, s, h]
        if h == 0:
            pre_g[...] += jnp.dot(rows, wg[wide, :], preferred_element_type=F32)
            pre_u[...] += jnp.dot(rows, wu[wide, :], preferred_element_type=F32)
        else:
            hid[...] += lax.dot_general(rows, wd[:, wide], NT, preferred_element_type=F32)

    def part_of(t):
        wide = pl.ds(pl.multiple_of(t * W, W), W)
        return lax.dot_general(gg[...], wg[wide, :], NT, preferred_element_type=F32) + lax.dot_general(
            ug[...], wu[wide, :], NT, preferred_element_type=F32
        )

    def finish(s):
        for h in range(2):
            rows = pl.ds(h * half, half)
            total = own[s, rows]
            for j in range(1, X):
                b_copy(s, j, h).wait_recv()
                total = total + b_recv[s, j, rows].astype(F32)
            c_send[s, rows] = total.astype(BF16)

            @pl.when(s != me)
            def _():
                c_copy(s, h).start()

    def arrive(k, h):
        @pl.when(k < E)
        def _():
            s = nth(me, k, E)
            z_arrival(s, h).wait_recv()
            spread(s, h)

        @pl.when((k >= ahead_of) & (k + 1 < E))
        def _():
            z_copy(nth(me, k + 1, E), h).start()

    def chunk(k, _):
        s = nth(me, k, E)
        arrive(k + 1, 0)

        pre_g[...] = jnp.zeros_like(pre_g)
        pre_u[...] = jnp.zeros_like(pre_u)
        hid[...] = jnp.zeros_like(hid)

        def slice_step(h, i, _):
            @pl.when(i == 1)
            def _():
                core_arrival(s, h, mx).wait_recv()

            for j in range(1, X):
                src = lax.rem(mx - j + X, X)

                @pl.when(i == 1 + j)
                def _():
                    x_arrival(s, h, j).wait_recv()
                    core_copy(s, h, src).start()

                @pl.when(i == X + j)
                def _():
                    core_arrival(s, h, src).wait_recv()

            j = jnp.where(i < 2, 0, jnp.where(i <= X, i - 1, i - X))
            other = jnp.where(i < 2, i, jnp.where(i <= X, 0, 1))
            xi = lax.rem(mx - j + X, X)
            core = lax.rem(mc + other, 2)
            forward(s, h, xi * 2 + core)
            return 0

        lax.fori_loop(0, T, functools.partial(slice_step, 0), 0)

        @pl.when(k == 0)
        def _():
            arrive(1, 1)

        lax.fori_loop(0, T, functools.partial(slice_step, 1), 0)

        @pl.when(k == E - 2)
        def _():
            arrive(k + 1, 1)

        pg, pu, hg = pre_g[...], pre_u[...], hid[...]
        sigma = jax.nn.sigmoid(pg)
        gg[...] = (hg * pu * sigma * (1.0 + pg * (1.0 - sigma))).astype(BF16)
        ug[...] = (hg * pg * sigma).astype(BF16)

        def give(xi):
            a_send[s, xi] = part_of(xi * 2 + oc).astype(BF16)
            a_copy(s, xi).start()
            mine = part_of(xi * 2 + mc)
            a_copy(s, xi).wait_recv()
            return mine + a_recv[s, xi].astype(F32)

        def keep(j, _):
            b_send[s, j] = give(lax.rem(mx + j, X)).astype(BF16)
            for h in range(2):
                b_copy(s, j, h).start()
            return 0

        lax.fori_loop(1, X, keep, 0)
        @pl.when(k >= 1)
        def _():
            finish(nth(me, k - 1, E))

        own[s] = give(mx)

        @pl.when((k > 0) & (k < E - 2))
        def _():
            arrive(k + 1, 1)


        return 0

    lax.fori_loop(0, E, chunk, 0)
    finish(nth(me, E - 1, E))

    total = lax.dot_general(pt[me], c_send[me], TN, preferred_element_type=F32)
    for k in range(1, E):
        s = nth(me, k, E)
        for h in range(2):
            c_arrival(s, h).wait_recv()
        total = total + lax.dot_general(pt[s], c_recv[s], TN, preferred_element_type=F32)
    out_ref[...] = total.astype(BF16)

    def drain(s, _):
        for h in range(2):

            @pl.when(s != me)
            def _():
                z_copy(s, h).wait_send()
                c_copy(s, h).wait_send()

            for j in range(1, X):
                x_copy(s, h, j).wait_send()
                b_copy(s, j, h).wait_send()
            for xi in range(X):
                core_copy(s, h, xi).wait_send()
        for xi in range(X):
            a_copy(s, xi).wait_send()
        return 0

    lax.fori_loop(0, E, drain, 0)


def per_device(activations, out_grad, routes, gates, gate_weight, up_weight, down_weight):
    E = lax.axis_size("expert")
    T = lax.axis_size("tensor")
    X = T // 2
    tok, top = routes.shape
    W = activations.shape[1]
    D, FF = gate_weight.shape[1:]
    need = 3 * tok * top // (2 * E)
    cap = -(-need // 32) * 32
    vmem = pl.BlockSpec(memory_space=pltpu.VMEM)
    anywhere = pl.BlockSpec(memory_space=pl.ANY)
    dma = pltpu.SemaphoreType.DMA
    return pl.pallas_call(
        functools.partial(kernel, E, T, cap),
        out_shape=jax.ShapeDtypeStruct((tok, W), BF16),
        in_specs=[vmem] * 4 + [anywhere] * 3,
        out_specs=vmem,
        scratch_shapes=[
            pltpu.VMEM((D, FF), BF16),
            pltpu.VMEM((D, FF), BF16),
            pltpu.VMEM((FF, D), BF16),
            pltpu.VMEM((E, 2, cap, W), BF16),
            pltpu.VMEM((T, E, 2, cap, W), BF16),
            pltpu.VMEM((E, cap, tok), BF16),
            pltpu.VMEM((cap, FF), F32),
            pltpu.VMEM((cap, FF), F32),
            pltpu.VMEM((cap, FF), F32),
            pltpu.VMEM((cap, FF), BF16),
            pltpu.VMEM((cap, FF), BF16),
            pltpu.VMEM((E, cap, W), F32),
            pltpu.VMEM((E, X, cap, W), BF16),
            pltpu.VMEM((E, X, cap, W), BF16),
            pltpu.VMEM((E, X, cap, W), BF16),
            pltpu.VMEM((E, X, cap, W), BF16),
            pltpu.VMEM((E, cap, W), BF16),
            pltpu.VMEM((E, cap, W), BF16),
            dma((3,)),
            dma((2, E)), dma((2, E)),
            dma((2, X, E)), dma((2, X, E)),
            dma((2, X, E)), dma((2, X, E)),
            dma((X, E)), dma((X, E)),
            dma((2, X, E)), dma((2, X, E)),
            dma((2, E)), dma((2, E)),
        ],
        compiler_params=pltpu.CompilerParams(
            collective_id=0, has_side_effects=True, vmem_limit_bytes=62 * 1024 * 1024
        ),
        cost_estimate=pl.CostEstimate(
            flops=10 * E * cap * D * FF, bytes_accessed=6 * D * FF, transcendentals=E * cap * FF
        ),
    )(activations, out_grad, routes.T, gates.T, gate_weight[0], up_weight[0], down_weight[0])


def solution(mesh):
    return jax.shard_map(
        per_device,
        mesh=mesh,
        in_specs=(
            P(("group", "expert"), "tensor"),
            P(("group", "expert"), "tensor"),
            P(("group", "expert"), None),
            P(("group", "expert"), None),
            P("expert", None, "tensor"),
            P("expert", None, "tensor"),
            P("expert", "tensor", None),
        ),
        out_specs=P(("group", "expert"), "tensor"),
        check_vma=False,
    )
```

time: 132 us -> 124 us (0.939)
  Pallas kernels: 127 us -> 122 us
  local copies, waits for them, and re-layouts: 4.63 us -> 1.82 us
    pallas_call x1, Pallas kernels: 127 us -> 122 us  [per_device(): pl.pallas_call(functools.partial(kernel, E, T, cap), out_shape=jax.ShapeD...]
    unnamed x3 -> x1, local copies, waits for them, and re-layouts: 4.63 us -> 1.82 us
where the time goes in v2:
time: 124 us
  Pallas kernels  122 us (98%)
  local copies, waits for them, and re-layouts  1.82 us (1%)
    pallas_call x1, Pallas kernels, per_device(): pl.pallas_call(functools.partial(kernel, E, T, cap), out_shape=jax.ShapeD...  122 us

profile of v2, /device:TPU:0, one launch (start us, length us, event | category | flops | bytes accessed | tf_op | source)
XLA Modules:
  0.0 123.6 jit_solution(4667969561513189269)
XLA Ops:
  0.0 121.8 %shard_map.73 = bf16[128,1792]{1,0:T(8,128)(2,1)} custom-call(bf16[128,1792]{1,0:T(8,128)(2,1)} %x_ref.1, bf16[128,1792]{1,0:T(8,128)(2,1)} %d_ref.1, s32[2,128]{1,0:T(2,128)} %bitcast.8, f32[2,128]{1,0:T(2,128)} %bitcast.9, bf16[7168,512]{1,0:T(8,128)(2,1)} %bitcast.5, bf16[7168,512]{1,0:T(8,128)(2,1)} %bitcast.6, bf16[512,7168]{1,0:T(8,128)(2,1)} %bitcast.7), custom_call_target="tpu_custom_call" | custom-call | flops 14092861440 | bytes 22020096 | tf_op jit(solution)/shard_map/pallas_call | solution.py:347
  121.8 1.8 %copy.9 = bf16[128,1792]{1,0:T(8,128)(2,1)} copy(bf16[128,1792]{1,0:T(8,128)(2,1)} %shard_map.73) | data formatting | bytes 917504

commit v3 on v2

--- a/solution.py
+++ b/solution.py
@@ -127,9 +127,9 @@
         )
 
     def spread(s, h):
+        core_copy(s, h, mx).start()
         for j in range(1, X):
             x_copy(s, h, j).start()
-        core_copy(s, h, mx).start()
 
     def a_copy(s, xi):
         return pltpu.make_async_remote_copy(
@@ -258,6 +258,10 @@
             return 0
 
         lax.fori_loop(0, T, functools.partial(slice_step, 0), 0)
+        pg, pu = pre_g[...], pre_u[...]
+        sigma = jax.nn.sigmoid(pg)
+        pre_u[...] = pu * sigma * (1.0 + pg * (1.0 - sigma))
+        pre_g[...] = pg * sigma
 
         @pl.when(k == 0)
         def _():
@@ -269,10 +273,8 @@
         def _():
             arrive(k + 1, 1)
 
-        pg, pu, hg = pre_g[...], pre_u[...], hid[...]
-        sigma = jax.nn.sigmoid(pg)
-        gg[...] = (hg * pu * sigma * (1.0 + pg * (1.0 - sigma))).astype(BF16)
-        ug[...] = (hg * pg * sigma).astype(BF16)
+        gg[...] = (hid[...] * pre_u[...]).astype(BF16)
+        ug[...] = (hid[...] * pre_g[...]).astype(BF16)
 
         def give(xi):
             a_send[s, xi] = part_of(xi * 2 + oc).astype(BF16)

time: 124 us -> 124 us (level)
  no operation moved by 1% of the time
where the time goes in v3:
time: 124 us
  Pallas kernels  122 us (98%)
  local copies, waits for them, and re-layouts  1.82 us (1%)
    pallas_call x1, Pallas kernels, per_device(): pl.pallas_call(functools.partial(kernel, E, T, cap), out_shape=jax.ShapeD...  122 us

profile of v3, /device:TPU:0, one launch (start us, length us, event | category | flops | bytes accessed | tf_op | source)
XLA Modules:
  0.0 123.6 jit_solution(9139892784647500347)
XLA Ops:
  0.0 121.8 %shard_map.73 = bf16[128,1792]{1,0:T(8,128)(2,1)} custom-call(bf16[128,1792]{1,0:T(8,128)(2,1)} %x_ref.1, bf16[128,1792]{1,0:T(8,128)(2,1)} %d_ref.1, s32[2,128]{1,0:T(2,128)} %bitcast.8, f32[2,128]{1,0:T(2,128)} %bitcast.9, bf16[7168,512]{1,0:T(8,128)(2,1)} %bitcast.5, bf16[7168,512]{1,0:T(8,128)(2,1)} %bitcast.6, bf16[512,7168]{1,0:T(8,128)(2,1)} %bitcast.7), custom_call_target="tpu_custom_call" | custom-call | flops 14092861440 | bytes 22020096 | tf_op jit(solution)/shard_map/pallas_call | solution.py:349
  121.8 1.8 %copy.9 = bf16[128,1792]{1,0:T(8,128)(2,1)} copy(bf16[128,1792]{1,0:T(8,128)(2,1)} %shard_map.73) | data formatting | bytes 917504
